TPU v7x, 128 devices: a whole 4x4x4 slice. The times are simulated.
128 devices in a mesh: row: 16 (over y, x_hi, core), col: 8 (over z, x_lo).
Axes of the slice: x: 4 (x_hi: 2, x_lo: 2; x = x_hi * 2 + x_lo), y: 4, z: 4, core: 2. Of those that a mesh axis runs over, the one named last changes fastest.
Arguments:
- ks_matrix: float32 [6144, 6144], P('row', 'col'), as said below
- occupancy: int32 [48, 48], P('row', 'col'), may hold values from 0 to 1, as said below
Outputs:
- sign_estimate: float32 [6144, 6144], P('row', 'col')
Inputs may be any that keep to these rules, and one draw needn't show every extreme that they name: `occupancy`: symmetric; every block pair at most 2 blocks from the diagonal is kept. `ks_matrix`: symmetric, and zero outside the kept block pairs.
All inputs are finite; a program needn't handle non-finite values.
Results may differ from a plain program's by a relative error of at most 0.0045.
Values may be sent and summed in bfloat16 or wider, within the bound.
No kernel may reach another device: no remote copies, remote signals or barrier semaphores. Data moves between devices by JAX's collectives and lax.ppermute only.
A program may use at most 64 MiB of HBM per device.

v0:
```python
import jax
import jax.numpy as jnp
from jax import lax
from jax.sharding import PartitionSpec as P

STEPS = 2


def right_folder(right_panel, shard_piece):
    return jnp.dot(shard_piece, right_panel, preferred_element_type=jnp.float32)


def body(ks_matrix, occupancy):
    block_size = ks_matrix.shape[0] // occupancy.shape[0]
    occupied = jnp.repeat(
        jnp.repeat(occupancy.astype(jnp.float32), block_size, axis=0), block_size, axis=1
    )
    iterate = ks_matrix
    for newton_step in range(STEPS):
        iterate_half = iterate.astype(jnp.bfloat16)
        row_panel = lax.all_gather(iterate_half, "col", axis=1, tiled=True)
        column_panel = lax.all_gather(iterate_half, "row", axis=0, tiled=True)
        square = jnp.dot(row_panel, column_panel, preferred_element_type=jnp.float32)
        square_half = square.astype(jnp.bfloat16)
        cube_term = right_folder(
            column_panel, lax.all_gather(square_half, "col", axis=1, tiled=True)
        )
        iterate = occupied * (1.5 * iterate - 0.5 * cube_term)
    return iterate


def solution(mesh):
    return jax.shard_map(
        body,
        mesh=mesh,
        in_specs=(P("row", "col"), P("row", "col")),
        out_specs=P("row", "col"),
        check_vma=False,
    )
```

profile of v0, /device:TPU:0, one launch (start us, length us, event | category | flops | bytes accessed | tf_op | source)
XLA Modules:
  0.0 615.5 jit_solution(12426676143898241168)
XLA Ops:
  6.5 0.0 all-gather.7.cloned.1.call-start
  6.5 2.1 convert_element_type.16
  8.7 0.0 all-gather.7.cloned.1.call-update
  8.7 0.0 all-gather.9.cloned.1.call-start
  8.8 0.7 all-gather.9.cloned.1.call-update
  9.5 0.0 copy-start.1
  9.5 0.0 copy-start
  9.5 0.0 all-gather.11.cloned.1.call-start
  9.5 102.6 %all-gather.7.cloned.1.call-done = bf16[384,6144]{1,0:T(8,128)(2,1)} async-done(((bf16[384,768]{1,0:T(8,128)(2,1)}), bf16[384,6144]{1,0:T(8,128)(2,1)}) %all-gather.7.cloned.1.call-update) | async-done | bytes 4718608 | tf_op jit(solution)/shard_map/all_gather | solution.py:21
  112.1 79.8 %all-gather.9.cloned.1.call-done = bf16[6144,768]{1,0:T(8,128)(2,1)} async-done(((bf16[384,768]{1,0:T(8,128)(2,1)}), bf16[6144,768]{1,0:T(8,128)(2,1)}) %all-gather.9.cloned.1.call-update) | async-done | bytes 9437200 | tf_op jit(solution)/shard_map/all_gather | solution.py:22
  191.9 9.7 %convolution_convert_fusion.1 = bf16[384,768]{1,0:T(8,128)(2,1)} fusion(bf16[384,6144]{1,0:T(8,128)(2,1)} %all-gather.7.cloned.1.call-done, bf16[6144,768]{1,0:T(8,128)(2,1)} %all-gather.9.cloned.1.call-done), kind=kOutput, calls=%fused_computation.7 | convolution fusion | flops 3624173568 | bytes 14745600 | tf_op jit(solution)/shard_map/dot_general | solution.py:23
  201.6 0.0 all-gather.11.cloned.1.call-update
  201.7 0.0 all-gather.13.cloned.1.call-start
  201.7 0.0 copy-done.1
  201.7 0.1 copy.3
  201.8 0.1 broadcast_bitcast_fusion
  201.9 0.1 broadcast_in_dim.7
  202.0 0.4 copy.5
  202.4 97.9 %all-gather.11.cloned.1.call-done = bf16[384,6144]{1,0:T(8,128)(2,1)} async-done(((bf16[384,768]{1,0:T(8,128)(2,1)}), bf16[384,6144]{1,0:T(8,128)(2,1)}) %all-gather.11.cloned.1.call-update) | async-done | bytes 4718608 | tf_op jit(solution)/shard_map/all_gather | solution.py:26
  300.2 0.0 copy-done
  300.2 9.8 %fusion.4 = (bf16[384,768]{1,0:T(8,128)(2,1)}, f32[384,768]{1,0:T(8,128)S(1)}) fusion(f32[384,768]{1,0:T(8,128)S(1)} %copy.5, bf16[384,6144]{1,0:T(8,128)(2,1)} %all-gather.11.cloned.1.call-done, bf16[6144,768]{1,0:T(8,128)(2,1)} %all-gather.9.cloned.1.call-done, f32[384,768]{1,0:T(8,128)S(1)} %copy-done), kind=kOutput, calls=%fused_computation.10 | convolution fusion | flops 3625353216 | bytes 18284544 | tf_op jit(solution)/shard_map/dot_general | solution.py:10
  310.0 0.0 all-gather.13.cloned.1.call-update
  310.0 0.0 all-gather.15.cloned.1.call-start
  310.1 0.5 all-gather.15.cloned.1.call-update
  310.6 0.2 all-gather.17.cloned.1.call-start
  310.9 99.9 %all-gather.13.cloned.1.call-done = bf16[384,6144]{1,0:T(8,128)(2,1)} async-done(((bf16[384,768]{1,0:T(8,128)(2,1)}), bf16[384,6144]{1,0:T(8,128)(2,1)}) %all-gather.13.cloned.1.call-update) | async-done | bytes 4718608 | tf_op jit(solution)/shard_map/all_gather | solution.py:21
  410.8 79.6 %all-gather.15.cloned.1.call-done = bf16[6144,768]{1,0:T(8,128)(2,1)} async-done(((bf16[384,768]{1,0:T(8,128)(2,1)}), bf16[6144,768]{1,0:T(8,128)(2,1)}) %all-gather.15.cloned.1.call-update) | async-done | bytes 9437200 | tf_op jit(solution)/shard_map/all_gather | solution.py:22
  490.4 9.7 %convolution_convert_fusion = bf16[384,768]{1,0:T(8,128)(2,1)} fusion(bf16[384,6144]{1,0:T(8,128)(2,1)} %all-gather.13.cloned.1.call-done, bf16[6144,768]{1,0:T(8,128)(2,1)} %all-gather.15.cloned.1.call-done), kind=kOutput, calls=%fused_computation.6 | convolution fusion | flops 3624173568 | bytes 14745600 | tf_op jit(solution)/shard_map/dot_general | solution.py:23
  500.2 0.0 all-gather.17.cloned.1.call-update
  500.2 98.6 %all-gather.17.cloned.1.call-done = bf16[384,6144]{1,0:T(8,128)(2,1)} async-done(((bf16[384,768]{1,0:T(8,128)(2,1)}), bf16[384,6144]{1,0:T(8,128)(2,1)}) %all-gather.17.cloned.1.call-update) | async-done | bytes 4718608 | tf_op jit(solution)/shard_map/all_gather | solution.py:26
  598.8 9.9 %fusion.3 = f32[384,768]{1,0:T(8,128)} fusion(f32[384,768]{1,0:T(8,128)S(1)} %copy.5, bf16[384,6144]{1,0:T(8,128)(2,1)} %all-gather.17.cloned.1.call-done, bf16[6144,768]{1,0:T(8,128)(2,1)} %all-gather.15.cloned.1.call-done, f32[384,768]{1,0:T(8,128)S(1)} %get-tuple-element.6), kind=kOutput, calls=%fused_computation.5 | convolution fusion | flops 3625058304 | bytes 17694720 | tf_op jit(solution)/shard_map/dot_general | solution.py:10
  (2 shorter events, 0.0 us)
Async XLA Ops:
  6.5 105.6 %all-gather.7.cloned.1.call-start = ((), (), s32[]{:S(2)}) async-start(), calls=%async_computation | async-start | bytes 5308416 | tf_op jit(solution)/shard_map/all_gather | solution.py:21
  8.7 183.2 %all-gather.9.cloned.1.call-start = ((), (), s32[]{:S(2)}) async-start(), calls=%async_computation.1 | async-start | bytes 10027008 | tf_op jit(solution)/shard_map/all_gather | solution.py:22
  9.5 192.3 %copy-start.1 = (s32[3,6]{1,0:T(4,128)S(1)}, s32[3,6]{1,0:T(4,128)}, u32[]{:S(2)}) copy-start(s32[3,6]{1,0:T(4,128)} %param.3) | copy-start | bytes 220
  9.5 290.8 %copy-start = (f32[384,768]{1,0:T(8,128)S(1)}, f32[384,768]{1,0:T(8,128)}, u32[]{:S(2)}) copy-start(f32[384,768]{1,0:T(8,128)} %param.2) | copy-start | bytes 3538948
  9.5 290.7 %all-gather.11.cloned.1.call-start = ((), (), s32[]{:S(2)}) async-start(), calls=%async_computation.2 | async-start | bytes 5308416 | tf_op jit(solution)/shard_map/all_gather | solution.py:26
  201.7 209.1 %all-gather.13.cloned.1.call-start = ((), (), s32[]{:S(2)}) async-start(), calls=%async_computation.3 | async-start | bytes 5308416 | tf_op jit(solution)/shard_map/all_gather | solution.py:21
  310.0 180.4 %all-gather.15.cloned.1.call-start = ((), (), s32[]{:S(2)}) async-start(), calls=%async_computation.4 | async-start | bytes 10027008 | tf_op jit(solution)/shard_map/all_gather | solution.py:22
  310.6 288.1 %all-gather.17.cloned.1.call-start = ((), (), s32[]{:S(2)}) async-start(), calls=%async_computation.5 | async-start | bytes 5308416 | tf_op jit(solution)/shard_map/all_gather | solution.py:26
Sparse Core Ops, SparseCore 0:
  9.0 103.0 all-gather.6
  114.6 77.2 all-gather.8
  201.8 98.3 all-gather.10
  310.2 100.5 all-gather.12
  413.1 77.2 all-gather.14
  500.3 98.3 all-gather.16
where the time goes:
time: 616 us
  waiting for transfers between devices  560 us (91%)
  matrix products  39.2 us (6%)
  between operations  13.5 us (2%)
    all_gather x2, waiting for transfers between devices, body(): row_panel = lax.all_gather(iterate_half, 'col', axis=1, tiled=True)  202 us
    all_gather x2, waiting for transfers between devices, body(): lax.all_gather(square_half, 'col', axis=1, tiled=True)  196 us
    all_gather x2, waiting for transfers between devices, body(): column_panel = lax.all_gather(iterate_half, 'row', axis=0, tiled=True)  159 us
    dot_general x2, matrix products, right_folder(): return jnp.dot(shard_piece, right_panel, preferred_element_type=jnp.float32)  19.7 us
    dot_general x2, matrix products, body(): jnp.dot(row_panel, column_panel, preferred_element_type=jnp.float32)  19.5 us
  transfers between devices with their start and end apart: 6, of which 6 were waited for; matrix products, arithmetic and copies ran while one was open for 0% of the time, Pallas kernels for 0%

commit v1 on v0

v1 whole, which is shorter than its diff:
```python
import functools
import itertools

import jax
import jax.numpy as jnp
from jax import lax
from jax.experimental import pallas as pl
from jax.experimental.pallas import tpu as pltpu
from jax.sharding import PartitionSpec as P

STEPS = 2
DIMS = (("y", 4), ("xh", 2), ("core", 2), ("z", 4), ("xl", 2))


def pairs(move):
    sizes = [n for _, n in DIMS]
    names = [name for name, _ in DIMS]

    def flat(place):
        index = 0
        for name, n in DIMS:
            index = index * n + place[name] % n
        return index

    out = []
    for coords in itertools.product(*map(range, sizes)):
        place = dict(zip(names, coords))
        out.append((flat(place), flat({**place, **move(place)})))
    return out


UP = {axis: pairs(lambda p, a=axis: {a: p[a] + 1}) for axis in ("y", "z")}
DOWN = {axis: pairs(lambda p, a=axis: {a: p[a] - 1}) for axis in ("y", "z")}
INNER = pairs(lambda p: {"xl": 1 - p["xl"]})
OUTER = pairs(lambda p: {"xh": 1 - p["xh"], "xl": 1 - p["xl"]})
CORE = pairs(lambda p: {"core": 1 - p["core"]})


def send(value, perm):
    return lax.ppermute(value, ("row", "col"), perm)


def ring(own, partner, axis):
    got = {(0, 0): own, (0, 1): partner}
    got[3, 0] = send(own, UP[axis])
    got[1, 0] = send(own, DOWN[axis])
    got[2, 0] = send(got[3, 0], UP[axis])
    got[1, 1] = send(partner, DOWN[axis])
    got[3, 1] = send(partner, UP[axis])
    got[2, 1] = send(got[1, 1], DOWN[axis])
    return got


ORDER = [(0, 0), (3, 0), (1, 0), (0, 1), (2, 0), (1, 1), (3, 1), (2, 1)]


def product_kernel(last, where, *refs):
    left, mine, other = refs[:8], refs[8:16], refs[16:24]
    refs = refs[24:]
    if last:
        old, occupancy, new, new_half = refs[:4]
        refs = refs[4:]
    else:
        square_half = refs[0]
        refs = refs[1:]
    left_buf, right_buf, total, left_sem, right_sem = refs[:5]
    shift, flip, core = where[0], where[1], where[2]
    rows, cols = total.shape
    lines = mine[0].shape[0]
    for n, (offset, pair) in enumerate(ORDER):
        pltpu.make_async_copy(left[n], left_buf.at[n], left_sem.at[n]).start()
        slot = 2 * lax.rem(offset - shift + 4, 4) + lax.rem(pair + flip, 2)
        for ref, half in ((mine[n], core), (other[n], 1 - core)):
            start = pl.multiple_of(half * lines, lines)
            pltpu.make_async_copy(
                ref, right_buf.at[slot, pl.ds(start, lines)], right_sem.at[slot]
            ).start()
    if last:
        old_buf, old_sem = refs[5:7]
        old_copy = pltpu.make_async_copy(old, old_buf, old_sem)
        old_copy.start()
    width = 256
    for n, (offset, pair) in enumerate(ORDER):
        slot = 2 * offset + pair
        pltpu.make_async_copy(left[n], left_buf.at[n], left_sem.at[n]).wait()
        pltpu.make_async_copy(
            right_buf.at[slot], right_buf.at[slot], right_sem.at[slot]
        ).wait()

        @pl.loop(0, cols // width)
        def _(j, n=n, slot=slot):
            where_j = pl.ds(pl.multiple_of(j * width, width), width)
            part = jnp.dot(
                left_buf[n], right_buf[slot, :, where_j], preferred_element_type=jnp.float32
            )
            if n == 0:
                total[:, where_j] = part
            else:
                total[:, where_j] += part

    if last:
        old_copy.wait()
        up, across = occupancy.shape
        block = rows // up
        for i in range(up):
            for j in range(across):
                at = (pl.ds(i * block, block), pl.ds(j * block, block))
                kept = occupancy[i, j].astype(jnp.float32)
                value = kept * (1.5 * old_buf[at] - 0.5 * total[at])
                new[at] = value
                new_half[at] = value.astype(jnp.bfloat16)
    else:
        square_half[...] = total[...].astype(jnp.bfloat16)


def product(where, left, mine, other, old=None, occupancy=None):
    last = old is not None
    rows, cols = left[0, 0].shape
    anywhere = pl.BlockSpec(memory_space=pl.ANY)
    vmem = pl.BlockSpec(memory_space=pltpu.VMEM)
    smem = pl.BlockSpec(memory_space=pltpu.SMEM)
    half = jax.ShapeDtypeStruct((rows, cols), jnp.bfloat16)
    scratch = [
        pltpu.VMEM((8, rows, cols), jnp.bfloat16),
        pltpu.VMEM((8, 2 * rows, cols), jnp.bfloat16),
        pltpu.VMEM((rows, cols), jnp.float32),
        pltpu.SemaphoreType.DMA((8,)),
        pltpu.SemaphoreType.DMA((8,)),
    ]
    operands = [where] + [b[at] for b in (left, mine, other) for at in ORDER]
    specs = [smem] + [anywhere] * 24
    shape, out_specs = half, vmem
    if last:
        operands += [old, occupancy]
        specs += [anywhere, smem]
        shape = (jax.ShapeDtypeStruct((rows, cols), jnp.float32), half)
        out_specs = (vmem, vmem)
        scratch += [pltpu.VMEM((rows, cols), jnp.float32), pltpu.SemaphoreType.DMA]
    return pl.pallas_call(
        functools.partial(product_kernel, last),
        out_shape=shape,
        in_specs=specs,
        out_specs=out_specs,
        scratch_shapes=scratch,
        compiler_params=pltpu.CompilerParams(vmem_limit_bytes=40 * 2**20),
        cost_estimate=pl.CostEstimate(
            flops=2 * rows * cols * 16 * rows,
            bytes_accessed=2 * 24 * rows * cols,
            transcendentals=0,
        ),
    )(*operands)


def body(ks_matrix, occupancy):
    row, col = lax.axis_index("row"), lax.axis_index("col")
    where = jnp.stack(
        [
            lax.rem(col // 2 - row // 4 + 4, 4),
            lax.rem(col + row // 2, 2),
            lax.rem(row, 2),
        ]
    ).astype(jnp.int32)
    iterate = ks_matrix
    half = iterate.astype(jnp.bfloat16)
    for _ in range(STEPS):
        beside = send(half, INNER)
        across = send(beside, OUTER)
        left = ring(half, beside, "z")
        mine = ring(half, across, "y")
        other = {at: send(block, CORE) for at, block in mine.items()}
        square_half = product(where, left, mine, other)
        left = ring(square_half, send(square_half, INNER), "z")
        iterate, half = product(where, left, mine, other, iterate, occupancy)
    return iterate


def solution(mesh):
    return jax.shard_map(
        body,
        mesh=mesh,
        in_specs=(P("row", "col"), P("row", "col")),
        out_specs=P("row", "col"),
        check_vma=False,
    )
```

time: 616 us -> 302 us (0.49)
  waiting for transfers between devices: 560 us -> 170 us
  starting transfers between devices: 0.38 us -> 67 us
  Pallas kernels: 0 us -> 47.4 us
  matrix products: 39.2 us -> 0 us
  local copies, waits for them, and re-layouts: 0.63 us -> 15.2 us
  between operations: 13.5 us -> 0.35 us
    all_gather x6 -> x0, waiting for transfers between devices: 558 us -> none  [the longest x2 202 us: body(): row_panel = lax.all_gather(iterate_half, 'col', axis=1, tiled=True)]
    ppermute x0 -> x58, waiting for transfers between devices: none -> 170 us  [send(): return lax.ppermute(value, ('row', 'col'), perm)]
    ppermute x0 -> x58, starting transfers between devices: none -> 67 us  [send(): return lax.ppermute(value, ('row', 'col'), perm)]
    pallas_call x0 -> x4, Pallas kernels: none -> 47.4 us  [product(): pl.pallas_call(functools.partial(product_kernel, last), out_shape=shape,...]
    dot_general x4 -> x0, matrix products: 39.2 us -> none  [the longest x2 19.7 us: right_folder(): return jnp.dot(shard_piece, right_panel, preferred_element_type=jnp.float32)]
    unnamed x6 -> x40, local copies, waits for them, and re-layouts: 0.09 us -> 15.2 us
  transfers between devices with their start and end apart: 6 -> 58, of which waited for: 6 -> 31; matrix products, arithmetic and copies ran while one was open for 0% -> 0% of each run, Pallas kernels for 0% -> 0%
where the time goes in v1:
time: 302 us; the launch traced here: 301 us
  waiting for transfers between devices  170 us (56%)
  starting transfers between devices  67 us (22%)
  Pallas kernels  47.4 us (16%)
  local copies, waits for them, and re-layouts  15.2 us (5%)
    ppermute x58, waiting for transfers between devices, send(): return lax.ppermute(value, ('row', 'col'), perm)  170 us
    ppermute x58, starting transfers between devices, send(): return lax.ppermute(value, ('row', 'col'), perm)  67 us
    pallas_call x4, Pallas kernels, product(): pl.pallas_call(functools.partial(product_kernel, last), out_shape=shape,...  47.4 us
    unnamed x40, local copies, waits for them, and re-layouts  15.2 us
  transfers between devices with their start and end apart: 58, of which 31 were waited for; matrix products, arithmetic and copies ran while one was open for 0% of the time, Pallas kernels for 0%

profile of v1, /device:TPU:0, one launch (start us, length us, event | category | flops | bytes accessed | tf_op | source)
XLA Modules:
  0.0 301.4 jit_solution(4503614781810310520)
XLA Ops:
  6.1 4.0 %collective-permute-start.1 = (bf16[384,768]{1,0:T(8,128)(2,1)S(1)}, bf16[384,768]{1,0:T(8,128)(2,1)S(1)}, u32[]{:S(2)}, u32[]{:S(2)}) collective-permute-start(bf16[384,768]{1,0:T(8,128)(2,1)S(1)} %convert_element_type.3.refs_0_.refs_8_), channel_id=1, source_target_pairs={{0,6},{1,7},{2,0},{3,1},{4,2},{5,3},{6,4},{7,5},{8,14},{9,15},{10,... | collective-permute-start | bytes 1769480 | tf_op jit(solution)/shard_map/ppermute | solution.py:40
  10.1 7.0 %collective-permute-done.2.refs_3_ = bf16[384,768]{1,0:T(8,128)(2,1)S(1)} collective-permute-done((bf16[384,768]{1,0:T(8,128)(2,1)S(1)}, bf16[384,768]{1,0:T(8,128)(2,1)S(1)}, u32[]{:S(2)}, u32[]{:S(2)}) %collective-permute-start.2) | collective-permute-done | bytes 589856 | tf_op jit(solution)/shard_map/ppermute | solution.py:40
  26.2 7.1 %collective-permute-done.9.refs_11_ = bf16[384,768]{1,0:T(8,128)(2,1)S(1)} collective-permute-done((bf16[384,768]{1,0:T(8,128)(2,1)S(1)}, bf16[384,768]{1,0:T(8,128)(2,1)S(1)}, u32[]{:S(2)}, u32[]{:S(2)}) %collective-permute-start.9) | collective-permute-done | bytes 589856 | tf_op jit(solution)/shard_map/ppermute | solution.py:40
  36.4 4.0 %collective-permute-start.4 = (bf16[384,768]{1,0:T(8,128)(2,1)S(1)}, bf16[384,768]{1,0:T(8,128)(2,1)}, u32[]{:S(2)}, u32[]{:S(2)}) collective-permute-start(bf16[384,768]{1,0:T(8,128)(2,1)S(1)} %collective-permute-done.2.refs_3_), channel_id=1, source_target_pairs={{0,6},{1,7},{2,0},{3,1},{4,2},{5,3},{6,4},{7,5},{8,14},{9,15},{10,... | collective-permute-start | bytes 1769480 | tf_op jit(solution)/shard_map/ppermute | solution.py:40
  44.6 3.3 %collective-permute-done.11.refs_13_ = bf16[384,768]{1,0:T(8,128)(2,1)} collective-permute-done((bf16[384,768]{1,0:T(8,128)(2,1)S(1)}, bf16[384,768]{1,0:T(8,128)(2,1)}, u32[]{:S(2)}, u32[]{:S(2)}) %collective-permute-start.11) | collective-permute-done | bytes 589856 | tf_op jit(solution)/shard_map/ppermute | solution.py:40
  47.8 3.8 %collective-permute-start.13 = (bf16[384,768]{1,0:T(8,128)(2,1)}, bf16[384,768]{1,0:T(8,128)(2,1)}, u32[]{:S(2)}, u32[]{:S(2)}) collective-permute-start(bf16[384,768]{1,0:T(8,128)(2,1)} %collective-permute-done.11.refs_13_), channel_id=1, source_target_pairs={{0,96},{1,97},{2,98},{3,99},{4,100},{5,101},{6,102},{7,103},{8,104... | collective-permute-start | bytes 1769480 | tf_op jit(solution)/shard_map/ppermute | solution.py:40
  51.6 5.1 %collective-permute-done.3.refs_4_ = bf16[384,768]{1,0:T(8,128)(2,1)S(1)} collective-permute-done((bf16[384,768]{1,0:T(8,128)(2,1)S(1)}, bf16[384,768]{1,0:T(8,128)(2,1)S(1)}, u32[]{:S(2)}, u32[]{:S(2)}) %collective-permute-start.3) | collective-permute-done | bytes 589856 | tf_op jit(solution)/shard_map/ppermute | solution.py:40
  58.4 3.2 %collective-permute-done.12.refs_14_ = bf16[384,768]{1,0:T(8,128)(2,1)} collective-permute-done((bf16[384,768]{1,0:T(8,128)(2,1)S(1)}, bf16[384,768]{1,0:T(8,128)(2,1)}, u32[]{:S(2)}, u32[]{:S(2)}) %collective-permute-start.12) | collective-permute-done | bytes 589856 | tf_op jit(solution)/shard_map/ppermute | solution.py:40
  62.6 7.8 %collective-permute-done.6.refs_7_ = bf16[384,768]{1,0:T(8,128)(2,1)} collective-permute-done((bf16[384,768]{1,0:T(8,128)(2,1)}, bf16[384,768]{1,0:T(8,128)(2,1)}, u32[]{:S(2)}, u32[]{:S(2)}) %collective-permute-start.6) | collective-permute-done | bytes 589856 | tf_op jit(solution)/shard_map/ppermute | solution.py:40
  79.0 10.6 %shard_map.28.refs_0_ = bf16[384,768]{1,0:T(8,128)(2,1)S(1)} custom-call(s32[3]{0:T(128)S(1)} %pad_add_fusion.where, bf16[384,768]{1,0:T(8,128)(2,1)S(1)} %convert_element_type.3.refs_0_.refs_8_, bf16[384,768]{1,0:T(8,128)(2,1)S(1)} %copy-done.14, bf16[384,768]{1,0:T(8,128)(2,1)S(1)} %copy-done.12, bf16[384,768]{1,0:T(8,128)(2,1)S(1)} %copy-done.10, ...), custom_call_target="tpu_custom_call" | custom-call | flops 3623878656 | bytes 14155776 | tf_op jit(solution)/shard_map/pallas_call | solution.py:139
  91.4 11.7 %collective-permute-done.24.refs_3_ = bf16[384,768]{1,0:T(8,128)(2,1)S(1)} collective-permute-done((bf16[384,768]{1,0:T(8,128)(2,1)S(1)}, bf16[384,768]{1,0:T(8,128)(2,1)S(1)}, u32[]{:S(2)}, u32[]{:S(2)}) %collective-permute-start.24) | collective-permute-done | bytes 589856 | tf_op jit(solution)/shard_map/ppermute | solution.py:40
  103.1 3.9 %collective-permute-start.26 = (bf16[384,768]{1,0:T(8,128)(2,1)S(1)}, bf16[384,768]{1,0:T(8,128)(2,1)S(1)}, u32[]{:S(2)}, u32[]{:S(2)}) collective-permute-start(bf16[384,768]{1,0:T(8,128)(2,1)S(1)} %collective-permute-done.24.refs_3_), channel_id=1, source_target_pairs={{0,6},{1,7},{2,0},{3,1},{4,2},{5,3},{6,4},{7,5},{8,14},{9,15},{10,... | collective-permute-start | bytes 1769480 | tf_op jit(solution)/shard_map/ppermute | solution.py:40
  109.1 11.7 %collective-permute-done.26.refs_5_ = bf16[384,768]{1,0:T(8,128)(2,1)S(1)} collective-permute-done((bf16[384,768]{1,0:T(8,128)(2,1)S(1)}, bf16[384,768]{1,0:T(8,128)(2,1)S(1)}, u32[]{:S(2)}, u32[]{:S(2)}) %collective-permute-start.26) | collective-permute-done | bytes 589856 | tf_op jit(solution)/shard_map/ppermute | solution.py:40
  120.8 3.7 %collective-permute-start.28 = (bf16[384,768]{1,0:T(8,128)(2,1)S(1)}, bf16[384,768]{1,0:T(8,128)(2,1)S(1)}, u32[]{:S(2)}, u32[]{:S(2)}) collective-permute-start(bf16[384,768]{1,0:T(8,128)(2,1)S(1)} %collective-permute-done.26.refs_5_), channel_id=1, source_target_pairs={{0,6},{1,7},{2,0},{3,1},{4,2},{5,3},{6,4},{7,5},{8,14},{9,15},{10,... | collective-permute-start | bytes 1769480 | tf_op jit(solution)/shard_map/ppermute | solution.py:40
  124.5 8.9 %collective-permute-done.23.refs_2_ = bf16[384,768]{1,0:T(8,128)(2,1)S(1)} collective-permute-done((bf16[384,768]{1,0:T(8,128)(2,1)S(1)}, bf16[384,768]{1,0:T(8,128)(2,1)S(1)}, u32[]{:S(2)}, u32[]{:S(2)}) %collective-permute-start.23) | collective-permute-done | bytes 589856 | tf_op jit(solution)/shard_map/ppermute | solution.py:40
  135.0 7.9 %collective-permute-done.28.refs_7_ = bf16[384,768]{1,0:T(8,128)(2,1)S(1)} collective-permute-done((bf16[384,768]{1,0:T(8,128)(2,1)S(1)}, bf16[384,768]{1,0:T(8,128)(2,1)S(1)}, u32[]{:S(2)}, u32[]{:S(2)}) %collective-permute-start.28) | collective-permute-done | bytes 589856 | tf_op jit(solution)/shard_map/ppermute | solution.py:40
  142.9 12.0 %shard_map.29 = (f32[384,768]{1,0:T(8,128)}, bf16[384,768]{1,0:T(8,128)(2,1)S(1)}) custom-call(s32[3]{0:T(128)S(1)} %pad_add_fusion.where, bf16[384,768]{1,0:T(8,128)(2,1)S(1)} %shard_map.28.refs_0_, bf16[384,768]{1,0:T(8,128)(2,1)S(1)} %collective-permute-done.22.refs_1_, bf16[384,768]{1,0:T(8,128)(2,1)S(1)} %collective-permute-done.23.refs_2_, ...), custom_call_target="tpu_custom_call" | custom-call | flops 3623878656 | bytes 14155776 | tf_op jit(solution)/shard_map/pallas_call | solution.py:139
  159.1 4.7 %collective-permute-start.30 = (bf16[384,768]{1,0:T(8,128)(2,1)S(1)}, bf16[384,768]{1,0:T(8,128)(2,1)S(1)}, u32[]{:S(2)}, u32[]{:S(2)}) collective-permute-start(bf16[384,768]{1,0:T(8,128)(2,1)S(1)} %get-tuple-element.8.refs_0_.refs_8_), channel_id=1, source_target_pairs={{0,6},{1,7},{2,0},{3,1},{4,2},{5,3},{6,4},{7,5},{8,14},{9,15},{10,... | collective-permute-start | bytes 1769480 | tf_op jit(solution)/shard_map/ppermute | solution.py:40
  163.8 7.2 %collective-permute-done.31.refs_3_ = bf16[384,768]{1,0:T(8,128)(2,1)S(1)} collective-permute-done((bf16[384,768]{1,0:T(8,128)(2,1)S(1)}, bf16[384,768]{1,0:T(8,128)(2,1)S(1)}, u32[]{:S(2)}, u32[]{:S(2)}) %collective-permute-start.31) | collective-permute-done | bytes 589856 | tf_op jit(solution)/shard_map/ppermute | solution.py:40
  176.4 3.1 %collective-permute-done.29.refs_1_ = bf16[384,768]{1,0:T(8,128)(2,1)S(1)} collective-permute-done((bf16[384,768]{1,0:T(8,128)(2,1)S(1)}, bf16[384,768]{1,0:T(8,128)(2,1)S(1)}, u32[]{:S(2)}, u32[]{:S(2)}) %collective-permute-start.29) | collective-permute-done | bytes 589856 | tf_op jit(solution)/shard_map/ppermute | solution.py:40
  179.5 7.7 %collective-permute-done.38.refs_11_ = bf16[384,768]{1,0:T(8,128)(2,1)S(1)} collective-permute-done((bf16[384,768]{1,0:T(8,128)(2,1)S(1)}, bf16[384,768]{1,0:T(8,128)(2,1)S(1)}, u32[]{:S(2)}, u32[]{:S(2)}) %collective-permute-start.38) | collective-permute-done | bytes 589856 | tf_op jit(solution)/shard_map/ppermute | solution.py:40
  194.9 6.5 %collective-permute-done.40.refs_13_ = bf16[384,768]{1,0:T(8,128)(2,1)S(1)} collective-permute-done((bf16[384,768]{1,0:T(8,128)(2,1)S(1)}, bf16[384,768]{1,0:T(8,128)(2,1)S(1)}, u32[]{:S(2)}, u32[]{:S(2)}) %collective-permute-start.40) | collective-permute-done | bytes 589856 | tf_op jit(solution)/shard_map/ppermute | solution.py:40
  209.3 6.0 %collective-permute-done.42.refs_15_ = bf16[384,768]{1,0:T(8,128)(2,1)S(1)} collective-permute-done((bf16[384,768]{1,0:T(8,128)(2,1)S(1)}, bf16[384,768]{1,0:T(8,128)(2,1)S(1)}, u32[]{:S(2)}, u32[]{:S(2)}) %collective-permute-start.42) | collective-permute-done | bytes 589856 | tf_op jit(solution)/shard_map/ppermute | solution.py:40
  215.3 5.6 %collective-permute-done.35.refs_7_ = bf16[384,768]{1,0:T(8,128)(2,1)S(1)} collective-permute-done((bf16[384,768]{1,0:T(8,128)(2,1)S(1)}, bf16[384,768]{1,0:T(8,128)(2,1)S(1)}, u32[]{:S(2)}, u32[]{:S(2)}) %collective-permute-start.35) | collective-permute-done | bytes 589856 | tf_op jit(solution)/shard_map/ppermute | solution.py:40
  220.9 11.8 %shard_map.30.refs_0_ = bf16[384,768]{1,0:T(8,128)(2,1)S(1)} custom-call(s32[3]{0:T(128)S(1)} %pad_add_fusion.where, bf16[384,768]{1,0:T(8,128)(2,1)S(1)} %get-tuple-element.8.refs_0_.refs_8_, bf16[384,768]{1,0:T(8,128)(2,1)S(1)} %collective-permute-done.29.refs_1_, bf16[384,768]{1,0:T(8,128)(2,1)S(1)} %collective-permute-done.30.refs_2_, ...), custom_call_target="tpu_custom_call" | custom-call | flops 3623878656 | bytes 14155776 | tf_op jit(solution)/shard_map/pallas_call | solution.py:139
  235.0 12.7 %collective-permute-done.53.refs_3_ = bf16[384,768]{1,0:T(8,128)(2,1)S(1)} collective-permute-done((bf16[384,768]{1,0:T(8,128)(2,1)S(1)}, bf16[384,768]{1,0:T(8,128)(2,1)S(1)}, u32[]{:S(2)}, u32[]{:S(2)}) %collective-permute-start.53) | collective-permute-done | bytes 589856 | tf_op jit(solution)/shard_map/ppermute | solution.py:40
  247.7 3.7 %collective-permute-start.55 = (bf16[384,768]{1,0:T(8,128)(2,1)S(1)}, bf16[384,768]{1,0:T(8,128)(2,1)S(1)}, u32[]{:S(2)}, u32[]{:S(2)}) collective-permute-start(bf16[384,768]{1,0:T(8,128)(2,1)S(1)} %collective-permute-done.53.refs_3_), channel_id=1, source_target_pairs={{0,6},{1,7},{2,0},{3,1},{4,2},{5,3},{6,4},{7,5},{8,14},{9,15},{10,... | collective-permute-start | bytes 1769480 | tf_op jit(solution)/shard_map/ppermute | solution.py:40
  253.4 11.7 %collective-permute-done.55.refs_5_ = bf16[384,768]{1,0:T(8,128)(2,1)S(1)} collective-permute-done((bf16[384,768]{1,0:T(8,128)(2,1)S(1)}, bf16[384,768]{1,0:T(8,128)(2,1)S(1)}, u32[]{:S(2)}, u32[]{:S(2)}) %collective-permute-start.55) | collective-permute-done | bytes 589856 | tf_op jit(solution)/shard_map/ppermute | solution.py:40
  265.2 3.7 %collective-permute-start.57 = (bf16[384,768]{1,0:T(8,128)(2,1)S(1)}, bf16[384,768]{1,0:T(8,128)(2,1)S(1)}, u32[]{:S(2)}, u32[]{:S(2)}) collective-permute-start(bf16[384,768]{1,0:T(8,128)(2,1)S(1)} %collective-permute-done.55.refs_5_), channel_id=1, source_target_pairs={{0,6},{1,7},{2,0},{3,1},{4,2},{5,3},{6,4},{7,5},{8,14},{9,15},{10,... | collective-permute-start | bytes 1769480 | tf_op jit(solution)/shard_map/ppermute | solution.py:40
  268.9 8.9 %collective-permute-done.52.refs_2_ = bf16[384,768]{1,0:T(8,128)(2,1)S(1)} collective-permute-done((bf16[384,768]{1,0:T(8,128)(2,1)S(1)}, bf16[384,768]{1,0:T(8,128)(2,1)S(1)}, u32[]{:S(2)}, u32[]{:S(2)}) %collective-permute-start.52) | collective-permute-done | bytes 589856 | tf_op jit(solution)/shard_map/ppermute | solution.py:40
  279.0 9.2 %collective-permute-done.57.refs_7_ = bf16[384,768]{1,0:T(8,128)(2,1)S(1)} collective-permute-done((bf16[384,768]{1,0:T(8,128)(2,1)S(1)}, bf16[384,768]{1,0:T(8,128)(2,1)S(1)}, u32[]{:S(2)}, u32[]{:S(2)}) %collective-permute-start.57) | collective-permute-done | bytes 589856 | tf_op jit(solution)/shard_map/ppermute | solution.py:40
  288.2 13.0 %shard_map.31 = (f32[384,768]{1,0:T(8,128)}, bf16[384,768]{1,0:T(8,128)(2,1)}) custom-call(s32[3]{0:T(128)S(1)} %pad_add_fusion.where, bf16[384,768]{1,0:T(8,128)(2,1)S(1)} %shard_map.30.refs_0_, bf16[384,768]{1,0:T(8,128)(2,1)S(1)} %collective-permute-done.51.refs_1_, bf16[384,768]{1,0:T(8,128)(2,1)S(1)} %collective-permute-done.52.refs_2_, ...), custom_call_target="tpu_custom_call" | custom-call | flops 3623878656 | bytes 14155776 | tf_op jit(solution)/shard_map/pallas_call | solution.py:139
  (130 shorter events, 69.7 us)
Async XLA Ops:
  1.4 15.7 %collective-permute-start.2 = (bf16[384,768]{1,0:T(8,128)(2,1)S(1)}, bf16[384,768]{1,0:T(8,128)(2,1)S(1)}, u32[]{:S(2)}, u32[]{:S(2)}) collective-permute-start(bf16[384,768]{1,0:T(8,128)(2,1)S(1)} %convert_element_type.3.refs_0_.refs_8_), channel_id=1, source_target_pairs={{0,1},{1,0},{2,3},{3,2},{4,5},{5,4},{6,7},{7,6},{8,9},{9,8},{10,11... | collective-permute-start | bytes 1769480 | tf_op jit(solution)/shard_map/ppermute | solution.py:40
  3.1 16.9 %collective-permute-start.8 = (bf16[384,768]{1,0:T(8,128)(2,1)S(1)}, bf16[384,768]{1,0:T(8,128)(2,1)S(1)}, u32[]{:S(2)}, u32[]{:S(2)}) collective-permute-start(bf16[384,768]{1,0:T(8,128)(2,1)S(1)} %convert_element_type.3.refs_0_.refs_8_), channel_id=1, source_target_pairs={{0,96},{1,97},{2,98},{3,99},{4,100},{5,101},{6,102},{7,103},{8,104... | collective-permute-start | bytes 1769480 | tf_op jit(solution)/shard_map/ppermute | solution.py:40
  6.1 16.3 %collective-permute-start.7 = (bf16[384,768]{1,0:T(8,128)(2,1)S(1)}, bf16[384,768]{1,0:T(8,128)(2,1)S(1)}, u32[]{:S(2)}, u32[]{:S(2)}) collective-permute-start(bf16[384,768]{1,0:T(8,128)(2,1)S(1)} %convert_element_type.3.refs_0_.refs_8_), channel_id=1, source_target_pairs={{0,32},{1,33},{2,34},{3,35},{4,36},{5,37},{6,38},{7,39},{8,40},{9,... | collective-permute-start | bytes 1769480 | tf_op jit(solution)/shard_map/ppermute | solution.py:40
  6.1 16.7 %collective-permute-start.1 = (bf16[384,768]{1,0:T(8,128)(2,1)S(1)}, bf16[384,768]{1,0:T(8,128)(2,1)S(1)}, u32[]{:S(2)}, u32[]{:S(2)}) collective-permute-start(bf16[384,768]{1,0:T(8,128)(2,1)S(1)} %convert_element_type.3.refs_0_.refs_8_), channel_id=1, source_target_pairs={{0,6},{1,7},{2,0},{3,1},{4,2},{5,3},{6,4},{7,5},{8,14},{9,15},{10,... | collective-permute-start | bytes 1769480 | tf_op jit(solution)/shard_map/ppermute | solution.py:40
  10.1 16.0 %collective-permute-start = (bf16[384,768]{1,0:T(8,128)(2,1)S(1)}, bf16[384,768]{1,0:T(8,128)(2,1)S(1)}, u32[]{:S(2)}, u32[]{:S(2)}) collective-permute-start(bf16[384,768]{1,0:T(8,128)(2,1)S(1)} %convert_element_type.3.refs_0_.refs_8_), channel_id=1, source_target_pairs={{0,2},{1,3},{2,4},{3,5},{4,6},{5,7},{6,0},{7,1},{8,10},{9,11},{10,... | collective-permute-start | bytes 1769480 | tf_op jit(solution)/shard_map/ppermute | solution.py:40
  17.2 16.1 %collective-permute-start.9 = (bf16[384,768]{1,0:T(8,128)(2,1)S(1)}, bf16[384,768]{1,0:T(8,128)(2,1)S(1)}, u32[]{:S(2)}, u32[]{:S(2)}) collective-permute-start(bf16[384,768]{1,0:T(8,128)(2,1)S(1)} %collective-permute-done.2.refs_3_), channel_id=1, source_target_pairs={{0,17},{1,16},{2,19},{3,18},{4,21},{5,20},{6,23},{7,22},{8,25},{9,... | collective-permute-start | bytes 1769480 | tf_op jit(solution)/shard_map/ppermute | solution.py:40
  20.0 16.3 %collective-permute-start.16 = (bf16[384,768]{1,0:T(8,128)(2,1)S(1)}, bf16[384,768]{1,0:T(8,128)(2,1)S(1)}, u32[]{:S(2)}, u32[]{:S(2)}) collective-permute-start(bf16[384,768]{1,0:T(8,128)(2,1)S(1)} %collective-permute-done.8.refs_10_), channel_id=1, source_target_pairs={{0,8},{1,9},{2,10},{3,11},{4,12},{5,13},{6,14},{7,15},{8,0},{9,1},... | collective-permute-start | bytes 1769480 | tf_op jit(solution)/shard_map/ppermute | solution.py:40
  22.4 18.8 %collective-permute-start.15 = (bf16[384,768]{1,0:T(8,128)(2,1)S(1)}, bf16[384,768]{1,0:T(8,128)(2,1)S(1)}, u32[]{:S(2)}, u32[]{:S(2)}) collective-permute-start(bf16[384,768]{1,0:T(8,128)(2,1)S(1)} %collective-permute-done.7.refs_9_), channel_id=1, source_target_pairs={{0,8},{1,9},{2,10},{3,11},{4,12},{5,13},{6,14},{7,15},{8,0},{9,1},... | collective-permute-start | bytes 1769480 | tf_op jit(solution)/shard_map/ppermute | solution.py:40
  23.6 19.3 %collective-permute-start.10 = (bf16[384,768]{1,0:T(8,128)(2,1)S(1)}, bf16[384,768]{1,0:T(8,128)(2,1)S(1)}, u32[]{:S(2)}, u32[]{:S(2)}) collective-permute-start(bf16[384,768]{1,0:T(8,128)(2,1)S(1)} %collective-permute-done.7.refs_9_), channel_id=1, source_target_pairs={{0,32},{1,33},{2,34},{3,35},{4,36},{5,37},{6,38},{7,39},{8,40},{9,... | collective-permute-start | bytes 1769480 | tf_op jit(solution)/shard_map/ppermute | solution.py:40
  26.2 17.6 %collective-permute-start.5 = (bf16[384,768]{1,0:T(8,128)(2,1)S(1)}, bf16[384,768]{1,0:T(8,128)(2,1)S(1)}, u32[]{:S(2)}, u32[]{:S(2)}) collective-permute-start(bf16[384,768]{1,0:T(8,128)(2,1)S(1)} %collective-permute-done.2.refs_3_), channel_id=1, source_target_pairs={{0,2},{1,3},{2,4},{3,5},{4,6},{5,7},{6,0},{7,1},{8,10},{9,11},{10,... | collective-permute-start | bytes 1769480 | tf_op jit(solution)/shard_map/ppermute | solution.py:40
  44.6 17.1 %collective-permute-start.12 = (bf16[384,768]{1,0:T(8,128)(2,1)S(1)}, bf16[384,768]{1,0:T(8,128)(2,1)}, u32[]{:S(2)}, u32[]{:S(2)}) collective-permute-start(bf16[384,768]{1,0:T(8,128)(2,1)S(1)} %collective-permute-done.9.refs_11_), channel_id=1, source_target_pairs={{0,32},{1,33},{2,34},{3,35},{4,36},{5,37},{6,38},{7,39},{8,40},{9,... | collective-permute-start | bytes 1769480 | tf_op jit(solution)/shard_map/ppermute | solution.py:40
  90.6 18.4 %collective-permute-start.22 = (bf16[384,768]{1,0:T(8,128)(2,1)S(1)}, bf16[384,768]{1,0:T(8,128)(2,1)S(1)}, u32[]{:S(2)}, u32[]{:S(2)}) collective-permute-start(bf16[384,768]{1,0:T(8,128)(2,1)S(1)} %shard_map.28.refs_0_), channel_id=1, source_target_pairs={{0,2},{1,3},{2,4},{3,5},{4,6},{5,7},{6,0},{7,1},{8,10},{9,11},{10,... | collective-permute-start | bytes 1769480 | tf_op jit(solution)/shard_map/ppermute | solution.py:40
  103.1 17.7 %collective-permute-start.26 = (bf16[384,768]{1,0:T(8,128)(2,1)S(1)}, bf16[384,768]{1,0:T(8,128)(2,1)S(1)}, u32[]{:S(2)}, u32[]{:S(2)}) collective-permute-start(bf16[384,768]{1,0:T(8,128)(2,1)S(1)} %collective-permute-done.24.refs_3_), channel_id=1, source_target_pairs={{0,6},{1,7},{2,0},{3,1},{4,2},{5,3},{6,4},{7,5},{8,14},{9,15},{10,... | collective-permute-start | bytes 1769480 | tf_op jit(solution)/shard_map/ppermute | solution.py:40
  107.0 26.4 %collective-permute-start.23 = (bf16[384,768]{1,0:T(8,128)(2,1)S(1)}, bf16[384,768]{1,0:T(8,128)(2,1)S(1)}, u32[]{:S(2)}, u32[]{:S(2)}) collective-permute-start(bf16[384,768]{1,0:T(8,128)(2,1)S(1)} %shard_map.28.refs_0_), channel_id=1, source_target_pairs={{0,6},{1,7},{2,0},{3,1},{4,2},{5,3},{6,4},{7,5},{8,14},{9,15},{10,... | collective-permute-start | bytes 1769480 | tf_op jit(solution)/shard_map/ppermute | solution.py:40
  107.6 25.8 %collective-permute-start.27 = (bf16[384,768]{1,0:T(8,128)(2,1)S(1)}, bf16[384,768]{1,0:T(8,128)(2,1)S(1)}, u32[]{:S(2)}, u32[]{:S(2)}) collective-permute-start(bf16[384,768]{1,0:T(8,128)(2,1)S(1)} %collective-permute-done.24.refs_3_), channel_id=1, source_target_pairs={{0,2},{1,3},{2,4},{3,5},{4,6},{5,7},{6,0},{7,1},{8,10},{9,11},{10,... | collective-permute-start | bytes 1769480 | tf_op jit(solution)/shard_map/ppermute | solution.py:40
  109.0 26.0 %collective-permute-start.25 = (bf16[384,768]{1,0:T(8,128)(2,1)S(1)}, bf16[384,768]{1,0:T(8,128)(2,1)S(1)}, u32[]{:S(2)}, u32[]{:S(2)}) collective-permute-start(bf16[384,768]{1,0:T(8,128)(2,1)S(1)} %collective-permute-done.22.refs_1_), channel_id=1, source_target_pairs={{0,2},{1,3},{2,4},{3,5},{4,6},{5,7},{6,0},{7,1},{8,10},{9,11},{10,... | collective-permute-start | bytes 1769480 | tf_op jit(solution)/shard_map/ppermute | solution.py:40
  120.8 22.1 %collective-permute-start.28 = (bf16[384,768]{1,0:T(8,128)(2,1)S(1)}, bf16[384,768]{1,0:T(8,128)(2,1)S(1)}, u32[]{:S(2)}, u32[]{:S(2)}) collective-permute-start(bf16[384,768]{1,0:T(8,128)(2,1)S(1)} %collective-permute-done.26.refs_5_), channel_id=1, source_target_pairs={{0,6},{1,7},{2,0},{3,1},{4,2},{5,3},{6,4},{7,5},{8,14},{9,15},{10,... | collective-permute-start | bytes 1769480 | tf_op jit(solution)/shard_map/ppermute | solution.py:40
  155.0 15.9 %collective-permute-start.31 = (bf16[384,768]{1,0:T(8,128)(2,1)S(1)}, bf16[384,768]{1,0:T(8,128)(2,1)S(1)}, u32[]{:S(2)}, u32[]{:S(2)}) collective-permute-start(bf16[384,768]{1,0:T(8,128)(2,1)S(1)} %get-tuple-element.8.refs_0_.refs_8_), channel_id=1, source_target_pairs={{0,1},{1,0},{2,3},{3,2},{4,5},{5,4},{6,7},{7,6},{8,9},{9,8},{10,11... | collective-permute-start | bytes 1769480 | tf_op jit(solution)/shard_map/ppermute | solution.py:40
  157.0 16.0 %collective-permute-start.37 = (bf16[384,768]{1,0:T(8,128)(2,1)S(1)}, bf16[384,768]{1,0:T(8,128)(2,1)S(1)}, u32[]{:S(2)}, u32[]{:S(2)}) collective-permute-start(bf16[384,768]{1,0:T(8,128)(2,1)S(1)} %get-tuple-element.8.refs_0_.refs_8_), channel_id=1, source_target_pairs={{0,96},{1,97},{2,98},{3,99},{4,100},{5,101},{6,102},{7,103},{8,104... | collective-permute-start | bytes 1769480 | tf_op jit(solution)/shard_map/ppermute | solution.py:40
  158.9 16.3 %collective-permute-start.36 = (bf16[384,768]{1,0:T(8,128)(2,1)S(1)}, bf16[384,768]{1,0:T(8,128)(2,1)S(1)}, u32[]{:S(2)}, u32[]{:S(2)}) collective-permute-start(bf16[384,768]{1,0:T(8,128)(2,1)S(1)} %get-tuple-element.8.refs_0_.refs_8_), channel_id=1, source_target_pairs={{0,32},{1,33},{2,34},{3,35},{4,36},{5,37},{6,38},{7,39},{8,40},{9,... | collective-permute-start | bytes 1769480 | tf_op jit(solution)/shard_map/ppermute | solution.py:40
  159.1 17.0 %collective-permute-start.30 = (bf16[384,768]{1,0:T(8,128)(2,1)S(1)}, bf16[384,768]{1,0:T(8,128)(2,1)S(1)}, u32[]{:S(2)}, u32[]{:S(2)}) collective-permute-start(bf16[384,768]{1,0:T(8,128)(2,1)S(1)} %get-tuple-element.8.refs_0_.refs_8_), channel_id=1, source_target_pairs={{0,6},{1,7},{2,0},{3,1},{4,2},{5,3},{6,4},{7,5},{8,14},{9,15},{10,... | collective-permute-start | bytes 1769480 | tf_op jit(solution)/shard_map/ppermute | solution.py:40
  163.8 15.8 %collective-permute-start.29 = (bf16[384,768]{1,0:T(8,128)(2,1)S(1)}, bf16[384,768]{1,0:T(8,128)(2,1)S(1)}, u32[]{:S(2)}, u32[]{:S(2)}) collective-permute-start(bf16[384,768]{1,0:T(8,128)(2,1)S(1)} %get-tuple-element.8.refs_0_.refs_8_), channel_id=1, source_target_pairs={{0,2},{1,3},{2,4},{3,5},{4,6},{5,7},{6,0},{7,1},{8,10},{9,11},{10,... | collective-permute-start | bytes 1769480 | tf_op jit(solution)/shard_map/ppermute | solution.py:40
  170.9 16.3 %collective-permute-start.38 = (bf16[384,768]{1,0:T(8,128)(2,1)S(1)}, bf16[384,768]{1,0:T(8,128)(2,1)S(1)}, u32[]{:S(2)}, u32[]{:S(2)}) collective-permute-start(bf16[384,768]{1,0:T(8,128)(2,1)S(1)} %collective-permute-done.31.refs_3_), channel_id=1, source_target_pairs={{0,17},{1,16},{2,19},{3,18},{4,21},{5,20},{6,23},{7,22},{8,25},{9,... | collective-permute-start | bytes 1769480 | tf_op jit(solution)/shard_map/ppermute | solution.py:40
  173.1 16.0 %collective-permute-start.45 = (bf16[384,768]{1,0:T(8,128)(2,1)S(1)}, bf16[384,768]{1,0:T(8,128)(2,1)S(1)}, u32[]{:S(2)}, u32[]{:S(2)}) collective-permute-start(bf16[384,768]{1,0:T(8,128)(2,1)S(1)} %collective-permute-done.37.refs_10_), channel_id=1, source_target_pairs={{0,8},{1,9},{2,10},{3,11},{4,12},{5,13},{6,14},{7,15},{8,0},{9,1},... | collective-permute-start | bytes 1769480 | tf_op jit(solution)/shard_map/ppermute | solution.py:40
  175.2 17.0 %collective-permute-start.44 = (bf16[384,768]{1,0:T(8,128)(2,1)S(1)}, bf16[384,768]{1,0:T(8,128)(2,1)S(1)}, u32[]{:S(2)}, u32[]{:S(2)}) collective-permute-start(bf16[384,768]{1,0:T(8,128)(2,1)S(1)} %collective-permute-done.36.refs_9_), channel_id=1, source_target_pairs={{0,8},{1,9},{2,10},{3,11},{4,12},{5,13},{6,14},{7,15},{8,0},{9,1},... | collective-permute-start | bytes 1769480 | tf_op jit(solution)/shard_map/ppermute | solution.py:40
  176.1 16.2 %collective-permute-start.39 = (bf16[384,768]{1,0:T(8,128)(2,1)S(1)}, bf16[384,768]{1,0:T(8,128)(2,1)S(1)}, u32[]{:S(2)}, u32[]{:S(2)}) collective-permute-start(bf16[384,768]{1,0:T(8,128)(2,1)S(1)} %collective-permute-done.36.refs_9_), channel_id=1, source_target_pairs={{0,32},{1,33},{2,34},{3,35},{4,36},{5,37},{6,38},{7,39},{8,40},{9,... | collective-permute-start | bytes 1769480 | tf_op jit(solution)/shard_map/ppermute | solution.py:40
  233.7 19.7 %collective-permute-start.51 = (bf16[384,768]{1,0:T(8,128)(2,1)S(1)}, bf16[384,768]{1,0:T(8,128)(2,1)S(1)}, u32[]{:S(2)}, u32[]{:S(2)}) collective-permute-start(bf16[384,768]{1,0:T(8,128)(2,1)S(1)} %shard_map.30.refs_0_), channel_id=1, source_target_pairs={{0,2},{1,3},{2,4},{3,5},{4,6},{5,7},{6,0},{7,1},{8,10},{9,11},{10,... | collective-permute-start | bytes 1769480 | tf_op jit(solution)/shard_map/ppermute | solution.py:40
  247.7 17.5 %collective-permute-start.55 = (bf16[384,768]{1,0:T(8,128)(2,1)S(1)}, bf16[384,768]{1,0:T(8,128)(2,1)S(1)}, u32[]{:S(2)}, u32[]{:S(2)}) collective-permute-start(bf16[384,768]{1,0:T(8,128)(2,1)S(1)} %collective-permute-done.53.refs_3_), channel_id=1, source_target_pairs={{0,6},{1,7},{2,0},{3,1},{4,2},{5,3},{6,4},{7,5},{8,14},{9,15},{10,... | collective-permute-start | bytes 1769480 | tf_op jit(solution)/shard_map/ppermute | solution.py:40
  251.4 26.4 %collective-permute-start.52 = (bf16[384,768]{1,0:T(8,128)(2,1)S(1)}, bf16[384,768]{1,0:T(8,128)(2,1)S(1)}, u32[]{:S(2)}, u32[]{:S(2)}) collective-permute-start(bf16[384,768]{1,0:T(8,128)(2,1)S(1)} %shard_map.30.refs_0_), channel_id=1, source_target_pairs={{0,6},{1,7},{2,0},{3,1},{4,2},{5,3},{6,4},{7,5},{8,14},{9,15},{10,... | collective-permute-start | bytes 1769480 | tf_op jit(solution)/shard_map/ppermute | solution.py:40
  251.4 26.4 %collective-permute-start.56 = (bf16[384,768]{1,0:T(8,128)(2,1)S(1)}, bf16[384,768]{1,0:T(8,128)(2,1)S(1)}, u32[]{:S(2)}, u32[]{:S(2)}) collective-permute-start(bf16[384,768]{1,0:T(8,128)(2,1)S(1)} %collective-permute-done.53.refs_3_), channel_id=1, source_target_pairs={{0,2},{1,3},{2,4},{3,5},{4,6},{5,7},{6,0},{7,1},{8,10},{9,11},{10,... | collective-permute-start | bytes 1769480 | tf_op jit(solution)/shard_map/ppermute | solution.py:40
  253.4 25.6 %collective-permute-start.54 = (bf16[384,768]{1,0:T(8,128)(2,1)S(1)}, bf16[384,768]{1,0:T(8,128)(2,1)S(1)}, u32[]{:S(2)}, u32[]{:S(2)}) collective-permute-start(bf16[384,768]{1,0:T(8,128)(2,1)S(1)} %collective-permute-done.51.refs_1_), channel_id=1, source_target_pairs={{0,2},{1,3},{2,4},{3,5},{4,6},{5,7},{6,0},{7,1},{8,10},{9,11},{10,... | collective-permute-start | bytes 1769480 | tf_op jit(solution)/shard_map/ppermute | solution.py:40
  265.2 23.0 %collective-permute-start.57 = (bf16[384,768]{1,0:T(8,128)(2,1)S(1)}, bf16[384,768]{1,0:T(8,128)(2,1)S(1)}, u32[]{:S(2)}, u32[]{:S(2)}) collective-permute-start(bf16[384,768]{1,0:T(8,128)(2,1)S(1)} %collective-permute-done.55.refs_5_), channel_id=1, source_target_pairs={{0,6},{1,7},{2,0},{3,1},{4,2},{5,3},{6,4},{7,5},{8,14},{9,15},{10,... | collective-permute-start | bytes 1769480 | tf_op jit(solution)/shard_map/ppermute | solution.py:40
  (46 other events, 566.4 us)
